TPU v7x, 256 devices: a whole 4x4x8 slice. The times are simulated.
256 devices in a mesh: row: 8 (over z_hi, core), col: 32 (over z_lo, x, y).
Axes of the slice: x: 4, y: 4, z: 8 (z_hi: 4, z_lo: 2; z = z_hi * 2 + z_lo), core: 2. Of those that a mesh axis runs over, the one named last changes fastest.
Arguments:
- inputs: float32 [1024, 6144], P('col', 'row'), may hold values from -6 to 6
- in_weight: float32 [6144, 24576], P('row', 'col'), may hold values from -0.078125 to 0.078125
- in_bias: float32 [24576], P('col'), may hold values from -3 to 3
- out_weight: float32 [24576, 6144], P('col', 'row'), may hold values from -0.0390625 to 0.0390625
- out_grad: float32 [1024, 6144], P('col', 'row'), may hold values from -0.875 to 0.875
Outputs:
- outputs: float32 [1024, 6144], P('col', 'row')
- grad_in: float32 [1024, 6144], P('col', 'row')
- grad_w_in: float32 [6144, 24576], P('row', 'col')
- grad_bias: float32 [24576], P('col')
- grad_w_out: float32 [24576, 6144], P('col', 'row')
All inputs are finite; a program needn't handle non-finite values.
Results may differ from a plain program's by a relative error of at most 0.00011.
Values sent between devices are 32-bit elements; how exact they have to be, the bound alone decides.
A program may use at most 128 MiB of HBM per device.

v0:
```python
import jax
import jax.numpy as jnp
from jax import lax
from jax.sharding import PartitionSpec as P

inv_root_two = 0.7071067811865476
inv_root_two_pi = 0.3989422804014327


def gelu_parts(pre):
    cdf = 0.5 * (1.0 + lax.erf(pre * inv_root_two))
    activated = pre * cdf
    slopes = cdf + pre * jnp.exp(-0.5 * pre * pre) * inv_root_two_pi
    return (activated, slopes)


def contract(left, right, left_dim, right_dim):
    return lax.dot_general(
        left,
        right,
        (((left_dim,), (right_dim,)), ((), ())),
        precision=lax.Precision.HIGHEST,
        preferred_element_type=jnp.float32,
    )


def on_device(inputs, in_weight, in_bias, out_weight, out_grad):
    all_rows, all_grads = (
        lax.all_gather(inputs, "col", axis=0, tiled=True),
        lax.all_gather(out_grad, "col", axis=0, tiled=True),
    )
    pre_part = contract(all_rows, in_weight, 1, 0)
    activated, slopes = gelu_parts(lax.psum(pre_part, "row") + in_bias)
    grad_w_out = contract(activated, all_grads, 0, 0)
    grad_act_part = contract(all_grads, out_weight, 1, 1)
    grad_pre = lax.psum(grad_act_part, "row") * slopes
    grad_bias = jnp.sum(grad_pre, axis=0)
    grad_w_in = contract(all_rows, grad_pre, 0, 0)
    outputs = lax.psum_scatter(
        contract(activated, out_weight, 1, 0), "col", scatter_dimension=0, tiled=True
    )
    grad_in = lax.psum_scatter(
        contract(grad_pre, in_weight, 1, 1), "col", scatter_dimension=0, tiled=True
    )
    return (outputs, grad_in, grad_w_in, grad_bias, grad_w_out)


def solution(mesh):
    in_specs = (P("col", "row"), P("row", "col"), P("col"), P("col", "row"), P("col", "row"))
    out_specs = (P("col", "row"), P("col", "row"), P("row", "col"), P("col"), P("col", "row"))
    return jax.shard_map(
        on_device, mesh=mesh, in_specs=in_specs, out_specs=out_specs, check_vma=False
    )
```

profile of v0, /device:TPU:64, one launch (start us, length us, event | category | flops | bytes accessed | tf_op | source)
XLA Modules:
  0.0 851.5 jit_solution(5393784270587335685)
XLA Ops:
  7.2 0.0 copy-start
  7.2 0.0 all-gather.5.cloned.1.call-start
  7.2 0.7 all-gather.5.cloned.1.call-update
  7.9 0.0 all-gather.3.cloned.1.call-start
  8.0 0.7 all-gather.3.cloned.1.call-update
  8.7 0.0 all-reduce.3.cloned.1.call-start
  8.7 160.9 %all-gather.5.cloned.1.call-done = f32[1024,768]{1,0:T(8,128)} async-done(((f32[32,768]{1,0:T(8,128)}), f32[1024,768]{1,0:T(8,128)}) %all-gather.5.cloned.1.call-update) | async-done | bytes 3145744 | tf_op jit(solution)/shard_map/all_gather | solution.py:30
  169.6 0.0 copy-done
  169.6 10.6 %fusion.10 = f32[1024,768]{1,0:T(8,128)} fusion(f32[1024,768]{1,0:T(8,128)} %all-gather.5.cloned.1.call-done, f32[768,768]{1,0:T(8,128)S(1)} %copy-done), kind=kOutput, calls=%fused_computation.13 | convolution fusion | flops 7247757312 | bytes 8650752 | tf_op jit(solution)/shard_map/dot_general | solution.py:18
  180.2 149.5 %all-gather.3.cloned.1.call-done = f32[1024,768]{1,0:T(8,128)} async-done(((f32[32,768]{1,0:T(8,128)}), f32[1024,768]{1,0:T(8,128)}) %all-gather.3.cloned.1.call-update) | async-done | bytes 3145744 | tf_op jit(solution)/shard_map/all_gather | solution.py:29
  329.7 11.3 %fusion.9 = f32[1024,768]{1,0:T(8,128)} fusion(f32[1024,768]{1,0:T(8,128)} %all-gather.3.cloned.1.call-done, f32[768,768]{1,0:T(8,128)} %param.6), kind=kOutput, calls=%fused_computation.12 | convolution fusion | flops 7247757312 | bytes 8650752 | tf_op jit(solution)/shard_map/dot_general | solution.py:18
  341.0 0.0 copy-start.3
  341.0 0.0 all-reduce.3.cloned.1.call-update
  341.0 0.0 reduce-scatter.3.cloned.1.call-start
  341.0 155.1 %all-reduce.3.cloned.1.call-done = (f32[1024,768]{1,0:T(8,128)}, f32[1024,768]{1,0:T(8,128)}) async-done(((f32[1024,768]{1,0:T(8,128)}, f32[1024,768]{1,0:T(8,128)}), (f32[1024,768]{1,0:T(8,128)}, f32[1024,768]{1,0:T(8,128)})) %all-reduce.3.cloned.1.call-update) | async-done | bytes 6291472 | tf_op jit(solution)/shard_map/psum | solution.py:33
  496.2 0.0 copy-done.3
  496.2 11.0 %fusion.6 = f32[1024,768]{1,0:T(8,128)} fusion(f32[768,768]{1,0:T(8,128)S(1)} %copy-done, f32[1024,768]{1,0:T(8,128)} %get-tuple-element.10, f32[768]{0:T(1024)S(1)} %copy-done.3), kind=kOutput, calls=%fused_computation.10 | convolution fusion | flops 7251689472 | bytes 8653824 | tf_op jit(solution)/shard_map/dot_general | solution.py:18
  507.1 0.0 reduce-scatter.3.cloned.1.call-update
  507.2 0.2 reduce-scatter.5.cloned.1.call-start
  507.4 0.0 copy-start.2
  507.4 4.3 fusion.7
  511.7 0.0 copy-start.1
  511.7 1.7 copy-done.1
  513.4 0.0 copy-done.2
  513.4 9.3 %fusion.11 = f32[1024,768]{1,0:T(8,128)} fusion(f32[1024,768]{1,0:T(8,128)S(1)} %get-tuple-element.13, f32[768,768]{1,0:T(8,128)S(1)} %copy-done.2), kind=kOutput, calls=%fused_computation.14 | convolution fusion | flops 7247757312 | bytes 8650752 | tf_op jit(solution)/shard_map/dot_general | solution.py:18
  522.7 0.0 reduce-scatter.5.cloned.1.call-update
  522.7 11.7 %convolution_bitcast_fusion = f32[768,768]{0,1:T(8,128)} fusion(f32[1024,768]{1,0:T(8,128)} %copy-done.1, f32[1024,768]{1,0:T(8,128)} %all-gather.3.cloned.1.call-done), kind=kOutput, calls=%fused_computation.8 | convolution fusion | flops 7247757312 | bytes 8650752 | tf_op jit(solution)/shard_map/dot_general | solution.py:18
  534.4 3.0 copy.10
  537.5 11.9 %fusion.5 = f32[768,768]{1,0:T(8,128)} fusion(f32[1024,768]{1,0:T(8,128)} %all-gather.5.cloned.1.call-done, f32[1024,768]{1,0:T(8,128)} %get-tuple-element.10, f32[768]{0:T(1024)S(1)} %copy-done.3), kind=kOutput, calls=%fused_computation.9 | convolution fusion | flops 7251689472 | bytes 8653824 | tf_op jit(solution)/shard_map/dot_general | solution.py:18
  549.3 127.7 %reduce-scatter.3.cloned.1.call-done = f32[32,768]{1,0:T(8,128)} async-done(((f32[1024,768]{1,0:T(8,128)}), f32[32,768]{1,0:T(8,128)}) %reduce-scatter.3.cloned.1.call-update) | async-done | bytes 98320 | tf_op jit(solution)/shard_map/reduce_scatter | solution.py:39
  677.1 167.9 %reduce-scatter.5.cloned.1.call-done = f32[32,768]{1,0:T(8,128)} async-done(((f32[1024,768]{1,0:T(8,128)}), f32[32,768]{1,0:T(8,128)}) %reduce-scatter.5.cloned.1.call-update) | async-done | bytes 98320 | tf_op jit(solution)/shard_map/reduce_scatter | solution.py:42
Async XLA Ops:
  7.2 162.4 %copy-start = (f32[768,768]{1,0:T(8,128)S(1)}, f32[768,768]{1,0:T(8,128)}, u32[]{:S(2)}) copy-start(f32[768,768]{1,0:T(8,128)} %param.8) | copy-start | bytes 7077892
  7.2 162.4 %all-gather.5.cloned.1.call-start = ((), (), s32[]{:S(2)}) async-start(), calls=%async_computation.4 | async-start | bytes 3244032 | tf_op jit(solution)/shard_map/all_gather | solution.py:30
  7.9 321.8 %all-gather.3.cloned.1.call-start = ((), (), s32[]{:S(2)}) async-start(), calls=%async_computation.2 | async-start | bytes 3244032 | tf_op jit(solution)/shard_map/all_gather | solution.py:29
  8.7 487.5 %all-reduce.3.cloned.1.call-start = ((), (), s32[]{:S(2)}) async-start(), calls=%async_computation.6 | async-start | bytes 12582912 | tf_op jit(solution)/shard_map/psum | solution.py:33
  341.0 155.2 %copy-start.3 = (f32[768]{0:T(1024)S(1)}, f32[768]{0:T(1024)}, u32[]{:S(2)}) copy-start(f32[768]{0:T(1024)} %param.7) | copy-start | bytes 9220
  341.0 336.1 %reduce-scatter.3.cloned.1.call-start = ((), (), s32[]{:S(2)}) async-start(), calls=%async_computation.3 | async-start | bytes 3244032 | tf_op jit(solution)/shard_map/reduce_scatter | solution.py:39
  507.2 337.8 %reduce-scatter.5.cloned.1.call-start = ((), (), s32[]{:S(2)}) async-start(), calls=%async_computation.5 | async-start | bytes 3244032 | tf_op jit(solution)/shard_map/reduce_scatter | solution.py:42
  507.4 6.0 copy-start.2
  511.7 1.7 copy-start.1
Sparse Core Ops, SparseCore 0:
  9.8 159.7 all-gather.4
  171.4 158.2 all-gather.2
  341.1 155.0 all-reduce.2
  507.3 169.7 reduce-scatter.2
  680.2 164.7 reduce-scatter.4
where the time goes:
time: 852 us
  waiting for transfers between devices  763 us (90%)
  matrix products  65.7 us (8%)
  between operations  13.8 us (2%)
    reduce_scatter x1, waiting for transfers between devices, on_device(): lax.psum_scatter(contract(grad_pre, in_weight, 1, 1), 'col', scatter_dime...  168 us
    all_gather x1, waiting for transfers between devices, on_device(): lax.all_gather(out_grad, 'col', axis=0, tiled=True)  161 us
    psum x1, waiting for transfers between devices, on_device(): activated, slopes = gelu_parts(lax.psum(pre_part, 'row') + in_bias)  155 us
    all_gather x1, waiting for transfers between devices, on_device(): lax.all_gather(inputs, 'col', axis=0, tiled=True)  149 us
    reduce_scatter x1, waiting for transfers between devices, on_device(): lax.psum_scatter(contract(activated, out_weight, 1, 0), 'col', scatter_di...  128 us
    dot_general x6, matrix products, contract(): lax.dot_general(left, right, (((left_dim,), (right_dim,)), ((), ())), pre...  65.7 us
  transfers between devices with their start and end apart: 5, of which 5 were waited for; matrix products, arithmetic and copies ran while one was open for 6% of the time, Pallas kernels for 0%

commit v1 on v0

v1 whole, which is shorter than its diff:
```python
import jax
import jax.numpy as jnp
from jax import lax
from jax.experimental import pallas as pl
from jax.experimental.pallas import tpu as pltpu
from jax.sharding import PartitionSpec as P

MESH = pl.DeviceIdType.MESH
F32 = jnp.float32
BF16 = jnp.bfloat16

inv_root_two = 0.7071067811865476
inv_root_two_pi = 0.3989422804014327

UNITS = ((0, (0, 1)), (1, (0, 1)), (2, (0, 1)), (3, (0, 1)))
SCHEDULE = (
    "A0 0", "A0 1", "A0 2", "A0 3", "A1 0", "W 0", "A2 0", "A1 1", "W 1",
    "B 0", "C 0", "A2 1", "A1 2", "D 0", "B 1", "C 1", "A2 2", "A1 3", "E 0",
    "D 1", "B 2", "C 2", "A2 3", "F 0", "E 1", "D 2", "B 3", "C 3", "G 0", "M 0",
    "F 1", "E 2", "D 3", "N 0", "R 0", "G 1", "M 1", "F 2", "E 3", "S 0", "N 1", "R 1",
    "G 2", "M 2", "F 3", "S 1", "T 0", "N 2", "R 2", "G 3", "M 3", "S 2", "T 1", "R 3", "N 3",
    "S 3", "T 2", "T 3",
)
WIDTH = 768
TILE = 256


def split(value):
    high = value.astype(BF16)
    return high, (value - high.astype(F32)).astype(BF16)


def dot(left, right):
    return lax.dot_general(left, right, (((1,), (0,)), ((), ())), preferred_element_type=F32)


def dot3(left, left_at, right, right_at, columns):
    high, low = left[left_at, 0], left[left_at, 1]
    right_high, right_low = right[right_at, 0, :, columns], right[right_at, 1, :, columns]
    return dot(high, right_high) + (dot(high, right_low) + dot(low, right_high))


def tiles(body):
    @pl.loop(0, WIDTH // TILE)
    def _(step):
        body(pl.ds(pl.multiple_of(step * TILE, TILE), TILE))


def kernel(
    inputs, in_weight, in_bias, out_weight, out_grad,
    outputs, grad_in, grad_w_in, grad_bias, grad_w_out,
    wide, weights, left, turned, right, bias, bias_sum, results,
    local_sem, send_sem, recv_sem, *buffers,
):
    row, col = lax.axis_index("row"), lax.axis_index("col")
    zh, core = lax.div(row, 2), lax.rem(row, 2)
    zl, x, y = lax.div(col, 16), lax.rem(lax.div(col, 4), 4), lax.rem(col, 4)

    def device(dz=0, dc=0, dl=0, dx=0, dy=0):
        return (
            lax.rem(zh + dz, 4) * 2 + lax.rem(core + dc, 2),
            lax.rem(zl + dl, 2) * 16 + lax.rem(x + dx, 4) * 4 + lax.rem(y + dy, 4),
        )

    units = [tuple(buffers[8 * u : 8 * u + 8]) for u in range(len(UNITS))]
    count = [0, 0]
    sent = []
    waiting = {}

    def local(src, dst):
        copy = pltpu.make_async_copy(src, dst, local_sem.at[count[0]])
        count[0] += 1
        copy.start()
        return copy

    def send(key, src, dst, to):
        copy = pltpu.make_async_remote_copy(
            src, dst, send_sem.at[count[1]], recv_sem.at[count[1]], device_id=to, device_id_type=MESH
        )
        count[1] += 1
        copy.start()
        waiting[key] = copy
        sent.append(copy)

    def arrived(*key):
        waiting[key].wait_recv()

    barrier = pltpu.get_barrier_semaphore()
    partners = [
        device(dz=1), device(dz=3), device(dc=1), device(dl=1),
        device(dx=1), device(dx=2), device(dx=3), device(dy=1), device(dy=2), device(dy=3),
    ]
    for partner in partners:
        pl.semaphore_signal(barrier, 1, device_id=partner, device_id_type=MESH)

    weight_copies = [local(in_weight, wide.at[0]), local(out_weight, wide.at[1])]
    bias_copy = local(in_bias, bias)
    own_copies = {}
    for u, (block, planes) in enumerate(UNITS):
        gathered = units[u][0]
        for a, source in enumerate((inputs, out_grad)):
            own_copies[u, a] = local(source.at[block], gathered.at[a, y, x, zl])
    pl.semaphore_wait(barrier, len(partners))

    def shard(ref, lead, owner_core, owner):
        return ref.at[(*lead, owner_core * 2 + lax.div(owner, 2), pl.ds(lax.rem(owner, 2) * 2, 2))]

    def half(ref, lead, owner_core):
        return ref.at[(*lead, pl.ds(owner_core * 2, 2))]

    def part(ref, lead, owner):
        return ref.at[(*lead, lax.div(owner, 2), pl.ds(lax.rem(owner, 2) * 2, 2))]

    up, down = lax.rem(zh + 1, 4), lax.rem(zh + 3, 4)
    far = lax.rem(zh + 2, 4)

    def a0(u):
        gathered = units[u][0]
        for a, source in enumerate((inputs, out_grad)):
            send((u, "a0", a), source.at[UNITS[u][0]], gathered.at[a, y, x, zl], device(dl=1))

    def a1(u):
        gathered = units[u][0]
        for a in range(2):
            own_copies[u, a].wait()
            arrived(u, "a0", a)
            for o in range(1, 4):
                to = device(dx=o) if a == 0 else device(dy=o)
                block = gathered.at[a, y, x]
                send((u, "a1", a, o), block, block, to)

    def a2(u):
        gathered = units[u][0]
        for a in range(2):
            for o in range(1, 4):
                arrived(u, "a1", a, o)
            for o in range(1, 4):
                to = device(dy=o) if a == 0 else device(dx=o)
                block = gathered.at[0, y] if a == 0 else gathered.at[1, :, x]
                send((u, "a2", a, o), block, block, to)

    def prepare(which):
        weight_copies[which].wait()

        def body(columns):
            high, low = split(wide[which, :, columns])
            weights[which, 0, :, columns] = high
            weights[which, 1, :, columns] = low
            high, low = split(wide[which, :, columns].T)
            weights[2 + which, 0, columns, :] = high
            weights[2 + which, 1, columns, :] = low

        tiles(body)

    def flat(value):
        return value.reshape(-1, WIDTH)

    def project(u):
        gathered, partial, from_core = units[u][0], units[u][1], units[u][2]
        shape = partial.shape[1:-1]
        rows = shape[0] * shape[1] * shape[2] * shape[3]
        for a in range(2):
            for o in range(1, 4):
                arrived(u, "a2", a, o)
            high, low = split(flat(gathered[a]))
            left[0, 0, :rows] = high
            left[0, 1, :rows] = low

            def body(columns, a=a):
                value = dot3(left, 0, weights, 0 if a == 0 else 3, columns)
                partial[a, :, :, :, :, columns] = value.reshape(*shape, TILE)

            tiles(body)
            send((u, "b", a), half(partial, (a,), 1 - core), from_core.at[a], device(dc=1))

    def reduce_start(u):
        partial, from_core, ring = units[u][1], units[u][2], units[u][3]
        for a in range(2):
            arrived(u, "b", a)
            from_core[a] = from_core[a] + half(partial, (a,), core)[...]
        send((u, "c", 0), part(from_core, (0,), far), ring.at[0], device(dz=1))
        send((u, "c", 1), part(from_core, (1,), far), ring.at[1], device(dz=3))
        send((u, "c", 2), part(from_core, (1,), up), ring.at[2], device(dz=1))
        send((u, "c", 3), part(from_core, (0,), down), ring.at[3], device(dz=3))

    def reduce_relay(u):
        from_core, ring = units[u][2], units[u][3]
        arrived(u, "c", 0)
        ring[0] = ring[0] + part(from_core, (0,), up)[...]
        send((u, "d", 0), ring.at[0], ring.at[4], device(dz=1))
        arrived(u, "c", 1)
        ring[1] = ring[1] + part(from_core, (1,), down)[...]
        send((u, "d", 1), ring.at[1], ring.at[5], device(dz=3))

    def activate(u):
        from_core, ring, hidden = units[u][2], units[u][3], units[u][4]
        arrived(u, "c", 2)
        arrived(u, "c", 3)
        arrived(u, "d", 0)
        arrived(u, "d", 1)
        pre = flat(part(from_core, (0,), zh)[...] + (ring[3] + ring[4])) + bias[...]
        grad_act = flat(part(from_core, (1,), zh)[...] + (ring[2] + ring[5]))
        cdf = 0.5 * (1.0 + lax.erf(pre * inv_root_two))
        slopes = cdf + pre * jnp.exp(-0.5 * pre * pre) * inv_root_two_pi
        shape = ring.shape[1:]
        shard(hidden, (0,), core, zh)[...] = (pre * cdf).reshape(shape)
        shard(hidden, (1,), core, zh)[...] = (grad_act * slopes).reshape(shape)
        block = shard(hidden, (slice(None),), core, zh)
        send((u, "e", 0), block, block, device(dz=1))
        send((u, "e", 1), block, block, device(dz=3))
        send((u, "e", 2), block, block, device(dc=1))

    def gather_relay(u):
        hidden = units[u][4]
        arrived(u, "e", 0)
        block = shard(hidden, (0,), core, down)
        send((u, "f", 0), block, block, device(dz=1))
        arrived(u, "e", 1)
        block = shard(hidden, (1,), core, up)
        send((u, "f", 1), block, block, device(dz=3))
        block = shard(hidden, (slice(None),), core, down)
        send((u, "f", 2), block, block, device(dc=1))
        block = shard(hidden, (slice(None),), core, up)
        send((u, "f", 3), block, block, device(dc=1))

    def gather_last(u):
        hidden = units[u][4]
        for a in range(2):
            arrived(u, "f", a)
            block = shard(hidden, (a,), core, far)
            send((u, "g", a), block, block, device(dc=1))

    def expand(u):
        partial, hidden, first = units[u][1], units[u][4], units[u][5]
        shape = partial.shape[1:-1]
        rows = shape[0] * shape[1] * shape[2] * shape[3]
        arrived(u, "e", 2)
        arrived(u, "f", 2)
        arrived(u, "f", 3)
        arrived(u, "g", 0)
        arrived(u, "g", 1)
        for a in range(2):
            high, low = split(flat(hidden[a]))
            left[a, 0, :rows] = high
            left[a, 1, :rows] = low
            waiting[u, "b", a].wait_send()

            def body(columns, a=a):
                value = dot3(left, a, weights, 1 if a == 0 else 2, columns)
                partial[a, :, :, :, :, columns] = value.reshape(*shape, TILE)

            tiles(body)
            for o in range(1, 4):
                if a == 0:
                    block, to = partial.at[0, lax.rem(y + o, 4)], device(dy=o)
                else:
                    block, to = partial.at[1, :, lax.rem(x + o, 4)], device(dx=o)
                send((u, "r", a, o), block, first.at[a, o - 1], to)

    def weight_grads(u):
        gathered, hidden = units[u][0], units[u][4]
        rows = gathered.shape[1] * gathered.shape[2] * gathered.shape[3] * gathered.shape[4]
        high, low = split(flat(hidden[0]).T)
        turned[0, 0, :, :rows] = high
        turned[0, 1, :, :rows] = low
        high, low = split(flat(gathered[0]).T)
        turned[1, 0, :, :rows] = high
        turned[1, 1, :, :rows] = low
        high, low = split(flat(gathered[1]))
        right[0, :rows] = high
        right[1, :rows] = low
        total = jnp.sum(flat(hidden[1]), axis=0, keepdims=True)
        bias_sum[...] = total if u == 0 else bias_sum[...] + total

        def body(columns):
            for which in range(2):
                high, low = turned[which, 0, :, :rows], turned[which, 1, :, :rows]
                if which == 0:
                    right_high, right_low = right[0, :rows, columns], right[1, :rows, columns]
                else:
                    right_high, right_low = left[1, 0, :rows, columns], left[1, 1, :rows, columns]
                value = dot(high, right_high) + (dot(high, right_low) + dot(low, right_high))
                wide[which, :, columns] = value if u == 0 else wide[which, :, columns] + value

        tiles(body)

    def scatter_first(u):
        partial, first, second = units[u][1], units[u][5], units[u][6]
        for a in range(2):
            for o in range(1, 4):
                arrived(u, "r", a, o)
            own = partial[0, y] if a == 0 else partial[1, :, x]
            first[a, 0] = own + first[a, 0] + (first[a, 1] + first[a, 2])
            for o in range(1, 4):
                if a == 0:
                    block, to = first.at[0, 0, lax.rem(x + o, 4)], device(dx=o)
                else:
                    block, to = first.at[1, 0, lax.rem(y + o, 4)], device(dy=o)
                send((u, "s", a, o), block, second.at[a, o - 1], to)

    def scatter_second(u):
        first, second, third = units[u][5], units[u][6], units[u][7]
        for a in range(2):
            for o in range(1, 4):
                arrived(u, "s", a, o)
            own = first[0, 0, x] if a == 0 else first[1, 0, y]
            second[a, 0] = own + second[a, 0] + (second[a, 1] + second[a, 2])
            send((u, "t", a), second.at[a, 0, 1 - zl], third.at[a], device(dl=1))

    def scatter_last(u):
        second, third = units[u][6], units[u][7]
        block = UNITS[u][0]
        for a in range(2):
            arrived(u, "t", a)
            results[a, block] = second[a, 0, zl] + third[a]

    stages = {
        "A0": a0, "A1": a1, "A2": a2, "W": prepare, "B": project, "C": reduce_start, "D": reduce_relay,
        "E": activate, "F": gather_relay, "G": gather_last, "M": expand, "N": weight_grads,
        "R": scatter_first, "S": scatter_second, "T": scatter_last,
    }
    for entry in SCHEDULE:
        name, u = entry.split()
        if name == "C" and u == "0":
            bias_copy.wait()
        stages[name](int(u))

    finals = [
        local(wide.at[1], grad_w_in), local(wide.at[0], grad_w_out), local(bias_sum, grad_bias),
        local(results.at[0], outputs), local(results.at[1], grad_in),
    ]
    done = {id(waiting[u, "b", a]) for u in range(len(UNITS)) for a in range(2)}
    for copy in sent:
        if id(copy) not in done:
            copy.wait_send()
    for copy in finals:
        copy.wait()


def on_device(inputs, in_weight, in_bias, out_weight, out_grad):
    blocks = inputs.shape[0] // 8
    cut = (blocks, 8, WIDTH)
    buffers = []
    for _, planes in UNITS:
        n = len(planes)
        buffers += [
            pltpu.VMEM((2, 4, 4, n, 8, WIDTH), F32),
            pltpu.VMEM((2, 4, 4, n, 8, WIDTH), F32),
            pltpu.VMEM((2, 2, 4, n, 8, WIDTH), F32),
            pltpu.VMEM((6, 2, n, 8, WIDTH), F32),
            pltpu.VMEM((2, 4, 4, n, 8, WIDTH), F32),
            pltpu.VMEM((2, 3, 4, n, 8, WIDTH), F32),
            pltpu.VMEM((2, 3, n, 8, WIDTH), F32),
            pltpu.VMEM((2, 8, WIDTH), F32),
        ]
    copies = 45 * len(UNITS)
    anywhere = pl.BlockSpec(memory_space=pl.ANY)
    outputs, grad_in, grad_w_in, grad_bias, grad_w_out = pl.pallas_call(
        kernel,
        out_shape=(
            jax.ShapeDtypeStruct(cut, F32),
            jax.ShapeDtypeStruct(cut, F32),
            jax.ShapeDtypeStruct((WIDTH, WIDTH), F32),
            jax.ShapeDtypeStruct((1, WIDTH), F32),
            jax.ShapeDtypeStruct((WIDTH, WIDTH), F32),
        ),
        in_specs=[anywhere] * 5,
        out_specs=[anywhere] * 5,
        scratch_shapes=[
            pltpu.VMEM((2, WIDTH, WIDTH), F32),
            pltpu.VMEM((4, 2, WIDTH, WIDTH), BF16),
            pltpu.VMEM((2, 2, 256, WIDTH), BF16),
            pltpu.VMEM((2, 2, WIDTH, 256), BF16),
            pltpu.VMEM((2, 256, WIDTH), BF16),
            pltpu.VMEM((1, WIDTH), F32),
            pltpu.VMEM((1, WIDTH), F32),
            pltpu.VMEM((2, blocks, 8, WIDTH), F32),
            pltpu.SemaphoreType.DMA((16,)),
            pltpu.SemaphoreType.DMA((copies,)),
            pltpu.SemaphoreType.DMA((copies,)),
            *buffers,
        ],
        compiler_params=pltpu.CompilerParams(
            collective_id=0, has_side_effects=True, vmem_limit_bytes=60 * 2**20
        ),
        name="mlp",
    )(
        inputs.reshape(cut), in_weight, in_bias.reshape(1, WIDTH), out_weight, out_grad.reshape(cut)
    )
    flat = (blocks * 8, WIDTH)
    return outputs.reshape(flat), grad_in.reshape(flat), grad_w_in, grad_bias.reshape(WIDTH), grad_w_out


def solution(mesh):
    in_specs = (P("col", "row"), P("row", "col"), P("col"), P("col", "row"), P("col", "row"))
    out_specs = (P("col", "row"), P("col", "row"), P("row", "col"), P("col"), P("col", "row"))
    return jax.shard_map(
        on_device, mesh=mesh, in_specs=in_specs, out_specs=out_specs, check_vma=False
    )
```

time: 852 us -> 192 us (0.23)
  waiting for transfers between devices: 763 us -> 0 us
  Pallas kernels: 0 us -> 179 us
  matrix products: 65.7 us -> 0 us
  between operations: 13.8 us -> 0.64 us
    all_gather x2 -> x0, waiting for transfers between devices: 310 us -> none  [the longest x1 161 us: on_device(): lax.all_gather(out_grad, 'col', axis=0, tiled=True)]
    reduce_scatter x2 -> x0, waiting for transfers between devices: 296 us -> none  [the longest x1 168 us: on_device(): lax.psum_scatter(contract(grad_pre, in_weight, 1, 1), 'col', scatter_dime...]
    pallas_call x0 -> x1, Pallas kernels: none -> 179 us  [on_device(): pl.pallas_call(kernel, out_shape=(jax.ShapeDtypeStruct(cut, F32), jax.Sha...]
    psum x1 -> x0, waiting for transfers between devices: 155 us -> none  [on_device(): activated, slopes = gelu_parts(lax.psum(pre_part, 'row') + in_bias)]
    dot_general x6 -> x0, matrix products: 65.7 us -> none  [contract(): lax.dot_general(left, right, (((left_dim,), (right_dim,)), ((), ())), pre...]
  transfers between devices with their start and end apart: 5 -> 0, of which waited for: 5 -> 0; matrix products, arithmetic and copies ran while one was open for 6% -> 0% of each run, Pallas kernels for 0% -> 0%
where the time goes in v1:
time: 192 us; the launch traced here: 190 us
  Pallas kernels  179 us (93%)
  local copies, waits for them, and re-layouts  9.12 us (5%)
    pallas_call x1, Pallas kernels, on_device(): pl.pallas_call(kernel, out_shape=(jax.ShapeDtypeStruct(cut, F32), jax.Sha...  179 us
    unnamed x6, local copies, waits for them, and re-layouts  7.86 us

profile of v1, /device:TPU:64, one launch (start us, length us, event | category | flops | bytes accessed | tf_op | source)
XLA Modules:
  0.0 190.0 jit_solution(1291179378256211171)
XLA Ops:
  0.6 1.3 reshape.29.in_bias
  1.9 178.9 %mlp.1 = (f32[4,8,768]{2,1,0:T(8,128)}, f32[4,8,768]{2,1,0:T(8,128)}, f32[768,768]{1,0:T(8,128)}, f32[1,768]{1,0:T(1,128)}, f32[768,768]{1,0:T(8,128)}) custom-call(f32[4,8,768]{2,1,0:T(8,128)} %bitcast.6, f32[768,768]{1,0:T(8,128)} %in_weight.1, f32[1,768]{1,0:T(1,128)} %reshape.29.in_bias, f32[768,768]{1,0:T(8,128)} %out_weight.1, f32[4,8,768]{2,1,0:T(8,128)} %bitcast.7), custom_call_target="tpu_custom_call" | custom-call | tf_op jit(solution)/shard_map/mlp/pallas_call | solution.py:358
  180.9 1.3 reduce
  182.1 1.5 copy.14
  183.7 1.5 copy.15
  185.2 0.0 copy-start
  185.2 3.4 %copy.16 = f32[768,768]{1,0:T(8,128)} copy(f32[768,768]{1,0:T(8,128)} %get-tuple-element.22) | data formatting | bytes 4718592
  188.6 0.0 copy-done
  188.6 1.4 copy.17
Async XLA Ops:
  185.2 3.4 %copy-start = (f32[768,768]{1,0:T(8,128)S(1)}, f32[768,768]{1,0:T(8,128)}, u32[]{:S(2)}) copy-start(f32[768,768]{1,0:T(8,128)} %get-tuple-element.24) | copy-start | bytes 7077892

commit v2 on v1

--- a/solution.py
+++ b/solution.py
@@ -12,14 +12,16 @@
 inv_root_two = 0.7071067811865476
 inv_root_two_pi = 0.3989422804014327
 
-UNITS = ((0, (0, 1)), (1, (0, 1)), (2, (0, 1)), (3, (0, 1)))
+UNITS = ((0, (0,)), (0, (1,)), (1, (0, 1)), (2, (0, 1)), (3, (0,)), (3, (1,)))
 SCHEDULE = (
-    "A0 0", "A0 1", "A0 2", "A0 3", "A1 0", "W 0", "A2 0", "A1 1", "W 1",
-    "B 0", "C 0", "A2 1", "A1 2", "D 0", "B 1", "C 1", "A2 2", "A1 3", "E 0",
-    "D 1", "B 2", "C 2", "A2 3", "F 0", "E 1", "D 2", "B 3", "C 3", "G 0", "M 0",
-    "F 1", "E 2", "D 3", "N 0", "R 0", "G 1", "M 1", "F 2", "E 3", "S 0", "N 1", "R 1",
-    "G 2", "M 2", "F 3", "S 1", "T 0", "N 2", "R 2", "G 3", "M 3", "S 2", "T 1", "R 3", "N 3",
-    "S 3", "T 2", "T 3",
+    "A0 1", "W 1", "A0 0", "A1 1", "A1 0", "A0 2", "A2 1", "W 0", "A2 0", "A0 4", "B 1", "A0 3",
+    "C 1", "A1 3", "B 0", "A1 2", "A1 4", "C 0", "A2 2", "A0 5", "D 1", "D 0", "E 1", "E 0",
+    "B 2", "A2 3", "F 1", "C 2", "A1 5", "D 2", "B 3", "F 0", "C 3", "A2 4", "G 1", "G 0",
+    "E 2", "A2 5", "M 0", "B 5", "D 3", "F 2", "E 3", "B 4", "G 2", "M 1", "C 4", "M 2",
+    "R 0", "D 4", "F 3", "N 0", "N 1", "C 5", "E 4", "R 1", "R 2", "G 3", "S 1", "M 3",
+    "S 2", "D 5", "T 2", "T 1", "S 0", "F 4", "E 5", "G 4", "T 0", "M 4", "F 5", "N 2",
+    "G 5", "R 3", "R 4", "M 5", "S 3", "N 3", "R 5", "S 4", "N 4", "S 5", "T 4", "N 5",
+    "T 3", "T 5",
 )
 WIDTH = 768
 TILE = 256
@@ -34,8 +36,8 @@
     return lax.dot_general(left, right, (((1,), (0,)), ((), ())), preferred_element_type=F32)
 
 
-def dot3(left, left_at, right, right_at, columns):
-    high, low = left[left_at, 0], left[left_at, 1]
+def dot3(left, left_at, rows, right, right_at, columns):
+    high, low = left[left_at, 0, :rows], left[left_at, 1, :rows]
     right_high, right_low = right[right_at, 0, :, columns], right[right_at, 1, :, columns]
     return dot(high, right_high) + (dot(high, right_low) + dot(low, right_high))
 
@@ -49,7 +51,7 @@
 def kernel(
     inputs, in_weight, in_bias, out_weight, out_grad,
     outputs, grad_in, grad_w_in, grad_bias, grad_w_out,
-    wide, weights, left, turned, right, bias, bias_sum, results,
+    weights, left, turned, right, bias,
     local_sem, send_sem, recv_sem, *buffers,
 ):
     row, col = lax.axis_index("row"), lax.axis_index("col")
@@ -62,6 +64,8 @@
             lax.rem(zl + dl, 2) * 16 + lax.rem(x + dx, 4) * 4 + lax.rem(y + dy, 4),
         )
 
+    wide = (grad_w_out, grad_w_in)
+    results = (outputs, grad_in)
     units = [tuple(buffers[8 * u : 8 * u + 8]) for u in range(len(UNITS))]
     count = [0, 0]
     sent = []
@@ -73,17 +77,34 @@
         copy.start()
         return copy
 
-    def send(key, src, dst, to):
+    def inside(u):
+        planes = UNITS[u][1]
+        return None if len(planes) == 2 else zl == planes[0]
+
+    def outside(u):
+        planes = UNITS[u][1]
+        return None if len(planes) == 2 else zl != planes[0]
+
+    def place(u):
+        return zl if len(UNITS[u][1]) == 2 else 0
+
+    def when(condition, action):
+        if condition is None:
+            action()
+        else:
+            pl.when(condition)(action)
+
+    def send(key, src, dst, to, only=None):
         copy = pltpu.make_async_remote_copy(
             src, dst, send_sem.at[count[1]], recv_sem.at[count[1]], device_id=to, device_id_type=MESH
         )
         count[1] += 1
-        copy.start()
+        when(only, copy.start)
         waiting[key] = copy
-        sent.append(copy)
-
-    def arrived(*key):
-        waiting[key].wait_recv()
+        sent.append((copy, only))
+
+    def arrived(*key, only=None):
+        when(only, waiting[key].wait_recv)
 
     barrier = pltpu.get_barrier_semaphore()
     partners = [
@@ -93,13 +114,17 @@
     for partner in partners:
         pl.semaphore_signal(barrier, 1, device_id=partner, device_id_type=MESH)
 
-    weight_copies = [local(in_weight, wide.at[0]), local(out_weight, wide.at[1])]
+    weight_copies = [local(in_weight, wide[0]), local(out_weight, wide[1])]
     bias_copy = local(in_bias, bias)
     own_copies = {}
     for u, (block, planes) in enumerate(UNITS):
-        gathered = units[u][0]
         for a, source in enumerate((inputs, out_grad)):
-            own_copies[u, a] = local(source.at[block], gathered.at[a, y, x, zl])
+            own = pltpu.make_async_copy(
+                source.at[pl.ds(block * 8, 8)], units[u][0].at[a, y, x, place(u)], local_sem.at[count[0]]
+            )
+            count[0] += 1
+            when(inside(u), own.start)
+            own_copies[u, a] = own
     pl.semaphore_wait(barrier, len(partners))
 
     def shard(ref, lead, owner_core, owner):
@@ -117,13 +142,14 @@
     def a0(u):
         gathered = units[u][0]
         for a, source in enumerate((inputs, out_grad)):
-            send((u, "a0", a), source.at[UNITS[u][0]], gathered.at[a, y, x, zl], device(dl=1))
+            rows = source.at[pl.ds(UNITS[u][0] * 8, 8)]
+            send((u, "a0", a), rows, gathered.at[a, y, x, place(u)], device(dl=1), inside(u))
 
     def a1(u):
         gathered = units[u][0]
         for a in range(2):
-            own_copies[u, a].wait()
-            arrived(u, "a0", a)
+            when(inside(u), own_copies[u, a].wait)
+            arrived(u, "a0", a, only=outside(u))
             for o in range(1, 4):
                 to = device(dx=o) if a == 0 else device(dy=o)
                 block = gathered.at[a, y, x]
@@ -143,10 +169,10 @@
         weight_copies[which].wait()
 
         def body(columns):
-            high, low = split(wide[which, :, columns])
+            high, low = split(wide[which][:, columns])
             weights[which, 0, :, columns] = high
             weights[which, 1, :, columns] = low
-            high, low = split(wide[which, :, columns].T)
+            high, low = split(wide[which][:, columns].T)
             weights[2 + which, 0, columns, :] = high
             weights[2 + which, 1, columns, :] = low
 
@@ -163,11 +189,11 @@
             for o in range(1, 4):
                 arrived(u, "a2", a, o)
             high, low = split(flat(gathered[a]))
-            left[0, 0, :rows] = high
-            left[0, 1, :rows] = low
+            left[a, 0, :rows] = high
+            left[a, 1, :rows] = low
 
             def body(columns, a=a):
-                value = dot3(left, 0, weights, 0 if a == 0 else 3, columns)
+                value = dot3(left, a, rows, weights, 0 if a == 0 else 3, columns)
                 partial[a, :, :, :, :, columns] = value.reshape(*shape, TILE)
 
             tiles(body)
@@ -198,7 +224,7 @@
         arrived(u, "c", 3)
         arrived(u, "d", 0)
         arrived(u, "d", 1)
-        pre = flat(part(from_core, (0,), zh)[...] + (ring[3] + ring[4])) + bias[...]
+        pre = flat(part(from_core, (0,), zh)[...] + (ring[3] + ring[4])) + bias[...].reshape(1, WIDTH)
         grad_act = flat(part(from_core, (1,), zh)[...] + (ring[2] + ring[5]))
         cdf = 0.5 * (1.0 + lax.erf(pre * inv_root_two))
         slopes = cdf + pre * jnp.exp(-0.5 * pre * pre) * inv_root_two_pi
@@ -246,7 +272,7 @@
             waiting[u, "b", a].wait_send()
 
             def body(columns, a=a):
-                value = dot3(left, a, weights, 1 if a == 0 else 2, columns)
+                value = dot3(left, a, rows, weights, 1 if a == 0 else 2, columns)
                 partial[a, :, :, :, :, columns] = value.reshape(*shape, TILE)
 
             tiles(body)
@@ -266,21 +292,19 @@
         high, low = split(flat(gathered[0]).T)
         turned[1, 0, :, :rows] = high
         turned[1, 1, :, :rows] = low
-        high, low = split(flat(gathered[1]))
-        right[0, :rows] = high
-        right[1, :rows] = low
-        total = jnp.sum(flat(hidden[1]), axis=0, keepdims=True)
-        bias_sum[...] = total if u == 0 else bias_sum[...] + total
+        for a, value in enumerate((gathered[1], hidden[1])):
+            high, low = split(flat(value))
+            right[a, 0, :rows] = high
+            right[a, 1, :rows] = low
+        total = jnp.sum(flat(hidden[1]), axis=0)
+        grad_bias[...] = total if u == 0 else grad_bias[...] + total
 
         def body(columns):
             for which in range(2):
                 high, low = turned[which, 0, :, :rows], turned[which, 1, :, :rows]
-                if which == 0:
-                    right_high, right_low = right[0, :rows, columns], right[1, :rows, columns]
-                else:
-                    right_high, right_low = left[1, 0, :rows, columns], left[1, 1, :rows, columns]
+                right_high, right_low = right[which, 0, :rows, columns], right[which, 1, :rows, columns]
                 value = dot(high, right_high) + (dot(high, right_low) + dot(low, right_high))
-                wide[which, :, columns] = value if u == 0 else wide[which, :, columns] + value
+                wide[which][:, columns] = value if u == 0 else wide[which][:, columns] + value
 
         tiles(body)
 
@@ -305,14 +329,19 @@
                 arrived(u, "s", a, o)
             own = first[0, 0, x] if a == 0 else first[1, 0, y]
             second[a, 0] = own + second[a, 0] + (second[a, 1] + second[a, 2])
-            send((u, "t", a), second.at[a, 0, 1 - zl], third.at[a], device(dl=1))
+            other = 1 - zl if len(UNITS[u][1]) == 2 else 0
+            send((u, "t", a), second.at[a, 0, other], third.at[a], device(dl=1), outside(u))
 
     def scatter_last(u):
         second, third = units[u][6], units[u][7]
-        block = UNITS[u][0]
-        for a in range(2):
-            arrived(u, "t", a)
-            results[a, block] = second[a, 0, zl] + third[a]
+        rows = pl.ds(UNITS[u][0] * 8, 8)
+
+        def add():
+            for a in range(2):
+                arrived(u, "t", a)
+                results[a][rows] = second[a, 0, place(u)] + third[a]
+
+        when(inside(u), add)
 
     stages = {
         "A0": a0, "A1": a1, "A2": a2, "W": prepare, "B": project, "C": reduce_start, "D": reduce_relay,
@@ -325,21 +354,22 @@
             bias_copy.wait()
         stages[name](int(u))
 
-    finals = [
-        local(wide.at[1], grad_w_in), local(wide.at[0], grad_w_out), local(bias_sum, grad_bias),
-        local(results.at[0], outputs), local(results.at[1], grad_in),
-    ]
     done = {id(waiting[u, "b", a]) for u in range(len(UNITS)) for a in range(2)}
-    for copy in sent:
+    for copy, only in sent:
         if id(copy) not in done:
-            copy.wait_send()
-    for copy in finals:
+            when(only, copy.wait_send)
+
+
+def hand_over(*refs):
+    copies = [pltpu.make_async_copy(refs[i], refs[5 + i], refs[10].at[i]) for i in range(5)]
+    for copy in copies:
+        copy.start()
+    for copy in copies:
         copy.wait()
 
 
 def on_device(inputs, in_weight, in_bias, out_weight, out_grad):
-    blocks = inputs.shape[0] // 8
-    cut = (blocks, 8, WIDTH)
+    tokens = inputs.shape[0]
     buffers = []
     for _, planes in UNITS:
         n = len(planes)
@@ -355,40 +385,46 @@
         ]
     copies = 45 * len(UNITS)
     anywhere = pl.BlockSpec(memory_space=pl.ANY)
-    outputs, grad_in, grad_w_in, grad_bias, grad_w_out = pl.pallas_call(
+    in_vmem = pl.BlockSpec(memory_space=pltpu.VMEM)
+    in_hbm = pl.BlockSpec(memory_space=pltpu.HBM)
+    shapes = [
+        jax.ShapeDtypeStruct((tokens, WIDTH), F32),
+        jax.ShapeDtypeStruct((tokens, WIDTH), F32),
+        jax.ShapeDtypeStruct((WIDTH, WIDTH), F32),
+        jax.ShapeDtypeStruct((WIDTH,), F32),
+        jax.ShapeDtypeStruct((WIDTH, WIDTH), F32),
+    ]
+    made = pl.pallas_call(
         kernel,
-        out_shape=(
-            jax.ShapeDtypeStruct(cut, F32),
-            jax.ShapeDtypeStruct(cut, F32),
-            jax.ShapeDtypeStruct((WIDTH, WIDTH), F32),
-            jax.ShapeDtypeStruct((1, WIDTH), F32),
-            jax.ShapeDtypeStruct((WIDTH, WIDTH), F32),
-        ),
+        out_shape=[pltpu.VMEM(shape.shape, shape.dtype) for shape in shapes],
         in_specs=[anywhere] * 5,
-        out_specs=[anywhere] * 5,
+        out_specs=[in_vmem] * 5,
         scratch_shapes=[
-            pltpu.VMEM((2, WIDTH, WIDTH), F32),
             pltpu.VMEM((4, 2, WIDTH, WIDTH), BF16),
             pltpu.VMEM((2, 2, 256, WIDTH), BF16),
             pltpu.VMEM((2, 2, WIDTH, 256), BF16),
-            pltpu.VMEM((2, 256, WIDTH), BF16),
-            pltpu.VMEM((1, WIDTH), F32),
-            pltpu.VMEM((1, WIDTH), F32),
-            pltpu.VMEM((2, blocks, 8, WIDTH), F32),
-            pltpu.SemaphoreType.DMA((16,)),
+            pltpu.VMEM((2, 2, 256, WIDTH), BF16),
+            pltpu.VMEM((WIDTH,), F32),
+            pltpu.SemaphoreType.DMA((8 + 2 * len(UNITS),)),
             pltpu.SemaphoreType.DMA((copies,)),
             pltpu.SemaphoreType.DMA((copies,)),
             *buffers,
         ],
         compiler_params=pltpu.CompilerParams(
-            collective_id=0, has_side_effects=True, vmem_limit_bytes=60 * 2**20
+            collective_id=0, has_side_effects=True, vmem_limit_bytes=52 * 2**20
         ),
         name="mlp",
-    )(
-        inputs.reshape(cut), in_weight, in_bias.reshape(1, WIDTH), out_weight, out_grad.reshape(cut)
-    )
-    flat = (blocks * 8, WIDTH)
-    return outputs.reshape(flat), grad_in.reshape(flat), grad_w_in, grad_bias.reshape(WIDTH), grad_w_out
+    )(inputs, in_weight, in_bias, out_weight, out_grad)
+    outputs, grad_in, grad_w_in, grad_bias, grad_w_out = pl.pallas_call(
+        hand_over,
+        out_shape=shapes,
+        in_specs=[in_vmem] * 5,
+        out_specs=[in_hbm] * 5,
+        scratch_shapes=[pltpu.SemaphoreType.DMA((5,))],
+        compiler_params=pltpu.CompilerParams(vmem_limit_bytes=2**20),
+        name="hand_over",
+    )(*[pltpu.with_memory_space_constraint(value, pltpu.VMEM) for value in made])
+    return outputs, grad_in, grad_w_in, grad_bias, grad_w_out
 
 
 def solution(mesh):

time: 192 us -> 169 us (0.88)
  Pallas kernels: 179 us -> 167 us
  local copies, waits for them, and re-layouts: 9.12 us -> 0 us
    pallas_call x1 -> x2, Pallas kernels: 179 us -> 167 us  [the longest x1 165 us: on_device(): pl.pallas_call(kernel, out_shape=[pltpu.VMEM(shape.shape, shape.dtype) fo...]
    unnamed x6 -> x0, local copies, waits for them, and re-layouts: 7.86 us -> none
where the time goes in v2:
time: 169 us; the launch traced here: 168 us
  Pallas kernels  167 us (99%)
    pallas_call x1, Pallas kernels, on_device(): pl.pallas_call(kernel, out_shape=[pltpu.VMEM(shape.shape, shape.dtype) fo...  165 us

profile of v2, /device:TPU:64, one launch (start us, length us, event | category | flops | bytes accessed | tf_op | source)
XLA Modules:
  0.0 168.2 jit_solution(1534090953734447120)
XLA Ops:
  0.6 165.1 %mlp.1 = (f32[32,768]{1,0:T(8,128)S(1)}, f32[32,768]{1,0:T(8,128)S(1)}, f32[768,768]{1,0:T(8,128)S(1)}, f32[768]{0:T(1024)S(1)}, f32[768,768]{1,0:T(8,128)S(1)}) custom-call(f32[32,768]{1,0:T(8,128)} %inputs.1, f32[768,768]{1,0:T(8,128)} %in_weight.1, f32[768]{0:T(1024)} %in_bias.1, f32[768,768]{1,0:T(8,128)} %out_weight.1, f32[32,768]{1,0:T(8,128)} %out_grad.1), custom_call_target="tpu_custom_call" | custom-call | tf_op jit(solution)/shard_map/mlp/pallas_call | solution.py:397
  165.8 2.3 %hand_over.1 = (f32[32,768]{1,0:T(8,128)}, f32[32,768]{1,0:T(8,128)}, f32[768,768]{1,0:T(8,128)}, f32[768]{0:T(1024)}, f32[768,768]{1,0:T(8,128)}) custom-call(f32[32,768]{1,0:T(8,128)S(1)} %get-tuple-element.10.refs_0_, f32[32,768]{1,0:T(8,128)S(1)} %get-tuple-element.11.refs_1_, f32[768,768]{1,0:T(8,128)S(1)} %get-tuple-element.12.refs_2_, ...), custom_call_target="tpu_custom_call" | custom-call | tf_op jit(solution)/shard_map/hand_over/pallas_call | solution.py:418

commit v3 on v2

v3 whole, which is shorter than its diff:
```python
import jax
import jax.numpy as jnp
from jax import lax
from jax.experimental import pallas as pl
from jax.experimental.pallas import tpu as pltpu
from jax.sharding import PartitionSpec as P

MESH = pl.DeviceIdType.MESH
F32 = jnp.float32
BF16 = jnp.bfloat16

inv_root_two = 0.7071067811865476
inv_root_two_pi = 0.3989422804014327

UNITS = ((0, (0,)), (0, (1,)), (1, (0, 1)), (2, (0, 1)), (3, (0,)), (3, (1,)))
SCHEDULE = (
    "Z1 0", "Z0 1", "Z1 4", "W0 0", "Z1 1", "Z0 2", "X0 1", "X1 0", "Z0 0", "X1 1", "X1 4", "Z0 3",
    "Z1 2", "Z0 5", "Z1 3", "X0 2", "Z1 5", "X0 0", "Y1 0", "Y0 1", "Y0 0", "Y1 1", "X1 2", "X1 5",
    "W1 0", "X0 5", "B0 1", "Z0 4", "C0 1", "B1 0", "X0 3", "X0 4", "C1 0", "Y0 2", "B0 0", "B1 1",
    "C0 0", "D0 1", "D1 0", "Y0 5", "Y1 2", "Y0 3", "D0 0", "Y0 4", "C1 1", "Y1 4", "E0 1", "Y1 5",
    "D1 1", "E0 0", "E1 0", "B0 2", "C0 2", "B1 2", "F0 0", "B1 4", "E1 1", "X1 3", "F1 0", "C1 4",
    "B0 3", "C1 2", "F0 1", "H0 0", "H0 1", "B0 4", "F1 1", "G1 0", "Y1 3", "D0 2", "C0 3", "G0 0",
    "G0 1", "M0 0", "H1 0", "C0 4", "G1 1", "D1 2", "H1 1", "M0 1", "E0 2", "D0 3", "M1 0", "E1 2",
    "D1 4", "B1 3", "H0 2", "C1 3", "M1 1", "B0 5", "F0 2", "F1 2", "N0 1", "D0 4", "D1 3", "B1 5",
    "G1 2", "R0 1", "E0 3", "N1 1", "H1 2", "C0 5", "G0 2", "E1 3", "M0 2", "F0 3", "H0 3", "E0 4",
    "E1 4", "M1 2", "N1 2", "F1 3", "C1 5", "G0 3", "N0 2", "M0 3", "D0 5", "G1 3", "H1 4", "H1 3",
    "F1 4", "R0 0", "R0 2", "R1 2", "F0 4", "R1 0", "S0 1", "D1 5", "M1 3", "H0 4", "E0 5", "N0 3",
    "E1 5", "G0 4", "M0 4", "S0 2", "H0 5", "G1 4", "N1 3", "R0 3", "F0 5", "G0 5", "M1 4", "M0 5",
    "R1 3", "F1 5", "H1 5", "G1 5", "M1 5", "N0 5", "R0 5", "S1 0", "R1 4", "R1 1", "S0 0", "S0 3",
    "R0 4", "S1 2", "T0 2", "T0 1", "S1 3", "R1 5", "S1 4", "S0 4", "S1 1", "T1 0", "T0 0", "T0 3",
    "S0 5", "S1 5", "T1 4", "N1 5", "T0 4", "T1 2", "T1 1", "T0 5", "T1 3", "T1 5",
)
WIDTH = 768
TILE = 256
LAG = 40
STRAIGHT = (5,)


def split(value):
    high = value.astype(BF16)
    return high, (value - high.astype(F32)).astype(BF16)


def dot(left, right):
    return lax.dot_general(left, right, (((1,), (0,)), ((), ())), preferred_element_type=F32)


def dot3(left, left_at, rows, right, right_at, columns):
    high, low = left[left_at, 0, :rows], left[left_at, 1, :rows]
    right_high, right_low = right[right_at, 0, :, columns], right[right_at, 1, :, columns]
    return dot(high, right_high) + (dot(high, right_low) + dot(low, right_high))


def tiles(body):
    @pl.loop(0, WIDTH // TILE)
    def _(step):
        body(pl.ds(pl.multiple_of(step * TILE, TILE), TILE))


def kernel(
    inputs, in_weight, in_bias, out_weight, out_grad,
    outputs, grad_in, grad_w_in, grad_bias, grad_w_out,
    weights, left, turned, right, bias,
    local_sem, send_sem, recv_sem, *buffers,
):
    row, col = lax.axis_index("row"), lax.axis_index("col")
    zh, core = lax.div(row, 2), lax.rem(row, 2)
    zl, x, y = lax.div(col, 16), lax.rem(lax.div(col, 4), 4), lax.rem(col, 4)

    def device(dz=0, dc=0, dl=0, dx=0, dy=0):
        return (
            lax.rem(zh + dz, 4) * 2 + lax.rem(core + dc, 2),
            lax.rem(zl + dl, 2) * 16 + lax.rem(x + dx, 4) * 4 + lax.rem(y + dy, 4),
        )

    wide = (grad_w_out, grad_w_in)
    results = (outputs, grad_in)
    units = [tuple(buffers[8 * u : 8 * u + 8]) for u in range(len(UNITS))]
    count = [0, 0]
    sent = []
    now = [0]
    waiting = {}

    def local(src, dst):
        copy = pltpu.make_async_copy(src, dst, local_sem.at[count[0]])
        count[0] += 1
        copy.start()
        return copy

    def inside(u):
        planes = UNITS[u][1]
        return None if len(planes) == 2 else zl == planes[0]

    def outside(u):
        planes = UNITS[u][1]
        return None if len(planes) == 2 else zl != planes[0]

    def place(u):
        return zl if len(UNITS[u][1]) == 2 else 0

    def when(condition, action):
        if condition is None:
            action()
        else:
            pl.when(condition)(action)

    def send(key, src, dst, to, only=None):
        copy = pltpu.make_async_remote_copy(
            src, dst, send_sem.at[count[1]], recv_sem.at[count[1]], device_id=to, device_id_type=MESH
        )
        count[1] += 1
        when(only, copy.start)
        waiting[key] = copy
        sent.append((now[0], key, copy, only))

    def settle(until):
        while sent and sent[0][0] <= until:
            _, key, copy, only = sent.pop(0)
            if key[1] != "b":
                when(only, copy.wait_send)

    def arrived(*key, only=None):
        when(only, waiting[key].wait_recv)

    barrier = pltpu.get_barrier_semaphore()
    partners = [
        device(dz=1), device(dz=2), device(dz=3), device(dc=1), device(dl=1),
        device(dx=1), device(dx=2), device(dx=3), device(dy=1), device(dy=2), device(dy=3),
    ]
    for partner in partners:
        pl.semaphore_signal(barrier, 1, device_id=partner, device_id_type=MESH)

    own_copies = {}
    for u, (block, planes) in enumerate(UNITS):
        for a, source in enumerate((inputs, out_grad)):
            own = pltpu.make_async_copy(
                source.at[pl.ds(block * 8, 8)], units[u][0].at[a, y, x, place(u)], local_sem.at[count[0]]
            )
            count[0] += 1
            when(inside(u), own.start)
            own_copies[u, a] = own
    weight_copies = [local(in_weight, wide[0]), local(out_weight, wide[1])]
    bias_copy = local(in_bias, bias)
    pl.semaphore_wait(barrier, len(partners))

    def shard(ref, lead, owner_core, owner):
        return ref.at[(*lead, owner_core * 2 + lax.div(owner, 2), pl.ds(lax.rem(owner, 2) * 2, 2))]

    def half(ref, lead, owner_core):
        return ref.at[(*lead, pl.ds(owner_core * 2, 2))]

    def part(ref, lead, owner):
        return ref.at[(*lead, lax.div(owner, 2), pl.ds(lax.rem(owner, 2) * 2, 2))]

    up, down = lax.rem(zh + 1, 4), lax.rem(zh + 3, 4)
    far = lax.rem(zh + 2, 4)

    onward, back = (device(dz=1), device(dz=3)), (device(dz=3), device(dz=1))
    ahead, behind = (up, down), (down, up)

    def exchange(u, a):
        rows = (inputs, out_grad)[a].at[pl.ds(UNITS[u][0] * 8, 8)]
        send((u, "z", a), rows, units[u][0].at[a, y, x, place(u)], device(dl=1), inside(u))

    def gather_first(u, a):
        when(inside(u), own_copies[u, a].wait)
        arrived(u, "z", a, only=outside(u))
        block = units[u][0].at[a, y, x]
        for o in (1, 3, 2):
            send((u, "x", a, o), block, block, device(dx=o) if a == 0 else device(dy=o))

    def gather_second(u, a):
        for o in (1, 2, 3):
            arrived(u, "x", a, o)
        block = units[u][0].at[0, y] if a == 0 else units[u][0].at[1, :, x]
        for o in (1, 3, 2):
            send((u, "y", a, o), block, block, device(dy=o) if a == 0 else device(dx=o))

    def prepare(which):
        weight_copies[which].wait()

        def body(columns):
            high, low = split(wide[which][:, columns])
            weights[which, 0, :, columns] = high
            weights[which, 1, :, columns] = low
            high, low = split(wide[which][:, columns].T)
            weights[2 + which, 0, columns, :] = high
            weights[2 + which, 1, columns, :] = low

        tiles(body)

    def flat(value):
        return value.reshape(-1, WIDTH)

    def project(u, a):
        gathered, partial, from_core = units[u][0], units[u][1], units[u][2]
        shape = partial.shape[1:-1]
        rows = shape[0] * shape[1] * shape[2] * shape[3]
        for o in range(1, 4):
            arrived(u, "y", a, o)
        high, low = split(flat(gathered[a]))
        left[a, 0, :rows] = high
        left[a, 1, :rows] = low

        def body(columns):
            value = dot3(left, a, rows, weights, 0 if a == 0 else 3, columns)
            partial[a, :, :, :, :, columns] = value.reshape(*shape, TILE)

        tiles(body)
        send((u, "b", a), half(partial, (a,), 1 - core), from_core.at[a], device(dc=1))

    def reduce_start(u, a):
        partial, from_core, ring = units[u][1], units[u][2], units[u][3]
        arrived(u, "b", a)
        from_core[a] = from_core[a] + half(partial, (a,), core)[...]
        send((u, "relay", a), part(from_core, (a,), far), ring.at[a], onward[a])
        send((u, "direct", a), part(from_core, (a,), behind[a]), ring.at[3 - a], back[a])

    def reduce_relay(u, a):
        from_core, ring = units[u][2], units[u][3]
        arrived(u, "relay", a)
        ring[a] = ring[a] + part(from_core, (a,), ahead[a])[...]
        send((u, "relayed", a), ring.at[a], ring.at[4 + a], onward[a])

    def activate(u, a):
        from_core, ring, hidden = units[u][2], units[u][3], units[u][4]
        arrived(u, "direct", a)
        arrived(u, "relayed", a)
        total = flat(part(from_core, (a,), zh)[...] + (ring[3 - a] + ring[4 + a]))
        shape = ring.shape[1:]
        if a == 0:
            if u == first_activated:
                bias_copy.wait()
            pre = total + bias[...].reshape(1, WIDTH)
            cdf = 0.5 * (1.0 + lax.erf(pre * inv_root_two))
            slopes = cdf + pre * jnp.exp(-0.5 * pre * pre) * inv_root_two_pi
            shard(hidden, (0,), core, zh)[...] = (pre * cdf).reshape(shape)
            ring[3] = slopes.reshape(shape)
        else:
            shard(hidden, (1,), core, zh)[...] = total.reshape(shape) * ring[3]
        block = shard(hidden, (a,), core, zh)
        send((u, "on", a), block, block, onward[a])
        send((u, "back", a), block, block, back[a])
        send((u, "own", a), block, block, device(dc=1))
        if u in STRAIGHT:
            send((u, "far", a), block, block, device(dz=2))

    def spread_relay(u, a):
        arrived(u, "on", a)
        block = shard(units[u][4], (a,), core, behind[a])
        if u not in STRAIGHT:
            send((u, "far", a), block, block, onward[a])
        send((u, "pass on", a), block, block, device(dc=1))

    def spread_back(u, a):
        arrived(u, "back", a)
        block = shard(units[u][4], (a,), core, ahead[a])
        send((u, "pass back", a), block, block, device(dc=1))

    def spread_far(u, a):
        arrived(u, "far", a)
        block = shard(units[u][4], (a,), core, far)
        send((u, "pass far", a), block, block, device(dc=1))

    def expand(u, a):
        partial, hidden, first = units[u][1], units[u][4], units[u][5]
        shape = partial.shape[1:-1]
        rows = shape[0] * shape[1] * shape[2] * shape[3]
        for name in ("own", "pass on", "pass back", "pass far"):
            arrived(u, name, a)
        high, low = split(flat(hidden[a]))
        left[a, 0, :rows] = high
        left[a, 1, :rows] = low
        waiting[u, "b", a].wait_send()

        def body(columns):
            value = dot3(left, a, rows, weights, 1 if a == 0 else 2, columns)
            partial[a, :, :, :, :, columns] = value.reshape(*shape, TILE)

        tiles(body)
        for o in (1, 3, 2):
            if a == 0:
                block, to = partial.at[0, lax.rem(y + o, 4)], device(dy=o)
            else:
                block, to = partial.at[1, :, lax.rem(x + o, 4)], device(dx=o)
            send((u, "r", a, o), block, first.at[a, o - 1], to)

    def weight_grads(u, a):
        group = [v for v in range(u + 1) if UNITS[v][0] == UNITS[u][0]]
        rows, total = 0, 0.0
        for v in group:
            gathered, hidden = units[v][0], units[v][4]
            lefts, rights = (hidden[0], gathered[1]) if a == 0 else (gathered[0], hidden[1])
            span = slice(rows, rows + gathered.shape[1] * gathered.shape[2] * gathered.shape[3] * gathered.shape[4])
            high, low = split(flat(lefts).T)
            turned[a, 0, :, span] = high
            turned[a, 1, :, span] = low
            high, low = split(flat(rights))
            right[a, 0, span] = high
            right[a, 1, span] = low
            rows = span.stop
            if a == 1:
                total = total + jnp.sum(flat(rights), axis=0)
        first = group[0] == 0
        if a == 1:
            grad_bias[...] = total if first else grad_bias[...] + total

        def body(columns):
            high, low = turned[a, 0, :, :rows], turned[a, 1, :, :rows]
            right_high, right_low = right[a, 0, :rows, columns], right[a, 1, :rows, columns]
            value = dot(high, right_high) + (dot(high, right_low) + dot(low, right_high))
            wide[a][:, columns] = value if first else wide[a][:, columns] + value

        tiles(body)

    def scatter_first(u, a):
        partial, first, second = units[u][1], units[u][5], units[u][6]
        for o in range(1, 4):
            arrived(u, "r", a, o)
        own = partial[0, y] if a == 0 else partial[1, :, x]
        first[a, 0] = own + first[a, 0] + (first[a, 1] + first[a, 2])
        for o in (1, 3, 2):
            if a == 0:
                block, to = first.at[0, 0, lax.rem(x + o, 4)], device(dx=o)
            else:
                block, to = first.at[1, 0, lax.rem(y + o, 4)], device(dy=o)
            send((u, "s", a, o), block, second.at[a, o - 1], to)

    def scatter_second(u, a):
        first, second, third = units[u][5], units[u][6], units[u][7]
        for o in range(1, 4):
            arrived(u, "s", a, o)
        own = first[0, 0, x] if a == 0 else first[1, 0, y]
        second[a, 0] = own + second[a, 0] + (second[a, 1] + second[a, 2])
        other = 1 - zl if len(UNITS[u][1]) == 2 else 0
        send((u, "t", a), second.at[a, 0, other], third.at[a], device(dl=1), outside(u))

    def scatter_last(u, a):
        second, third = units[u][6], units[u][7]

        def add():
            arrived(u, "t", a)
            results[a][pl.ds(UNITS[u][0] * 8, 8)] = second[a, 0, place(u)] + third[a]

        when(inside(u), add)

    stages = {
        "Z": exchange, "X": gather_first, "Y": gather_second, "B": project, "C": reduce_start,
        "D": reduce_relay, "E": activate, "F": spread_relay, "H": spread_back, "G": spread_far,
        "M": expand, "N": weight_grads, "R": scatter_first, "S": scatter_second, "T": scatter_last,
    }
    first_activated = int(next(entry for entry in SCHEDULE if entry[:2] == "E0").split()[1])
    for step, entry in enumerate(SCHEDULE):
        now[0] = step
        name, u = entry.split()
        if name[0] == "W":
            prepare(int(name[1]))
        else:
            stages[name[0]](int(u), int(name[1]))
        settle(step - LAG)
    settle(len(SCHEDULE))


def hand_over(*refs):
    copies = [pltpu.make_async_copy(refs[i], refs[5 + i], refs[10].at[i]) for i in range(5)]
    for copy in copies:
        copy.start()
    for copy in copies:
        copy.wait()


def on_device(inputs, in_weight, in_bias, out_weight, out_grad):
    tokens = inputs.shape[0]
    buffers = []
    for _, planes in UNITS:
        n = len(planes)
        buffers += [
            pltpu.VMEM((2, 4, 4, n, 8, WIDTH), F32),
            pltpu.VMEM((2, 4, 4, n, 8, WIDTH), F32),
            pltpu.VMEM((2, 2, 4, n, 8, WIDTH), F32),
            pltpu.VMEM((6, 2, n, 8, WIDTH), F32),
            pltpu.VMEM((2, 4, 4, n, 8, WIDTH), F32),
            pltpu.VMEM((2, 3, 4, n, 8, WIDTH), F32),
            pltpu.VMEM((2, 3, n, 8, WIDTH), F32),
            pltpu.VMEM((2, 8, WIDTH), F32),
        ]
    copies = 50 * len(UNITS)
    anywhere = pl.BlockSpec(memory_space=pl.ANY)
    in_vmem = pl.BlockSpec(memory_space=pltpu.VMEM)
    in_hbm = pl.BlockSpec(memory_space=pltpu.HBM)
    shapes = [
        jax.ShapeDtypeStruct((tokens, WIDTH), F32),
        jax.ShapeDtypeStruct((tokens, WIDTH), F32),
        jax.ShapeDtypeStruct((WIDTH, WIDTH), F32),
        jax.ShapeDtypeStruct((WIDTH,), F32),
        jax.ShapeDtypeStruct((WIDTH, WIDTH), F32),
    ]
    made = pl.pallas_call(
        kernel,
        out_shape=[pltpu.VMEM(shape.shape, shape.dtype) for shape in shapes],
        in_specs=[anywhere] * 5,
        out_specs=[in_vmem] * 5,
        scratch_shapes=[
            pltpu.VMEM((4, 2, WIDTH, WIDTH), BF16),
            pltpu.VMEM((2, 2, 256, WIDTH), BF16),
            pltpu.VMEM((2, 2, WIDTH, 256), BF16),
            pltpu.VMEM((2, 2, 256, WIDTH), BF16),
            pltpu.VMEM((WIDTH,), F32),
            pltpu.SemaphoreType.DMA((8 + 2 * len(UNITS),)),
            pltpu.SemaphoreType.DMA((copies,)),
            pltpu.SemaphoreType.DMA((copies,)),
            *buffers,
        ],
        compiler_params=pltpu.CompilerParams(
            collective_id=0, has_side_effects=True, vmem_limit_bytes=52 * 2**20
        ),
        name="mlp",
    )(inputs, in_weight, in_bias, out_weight, out_grad)
    outputs, grad_in, grad_w_in, grad_bias, grad_w_out = pl.pallas_call(
        hand_over,
        out_shape=shapes,
        in_specs=[in_vmem] * 5,
        out_specs=[in_hbm] * 5,
        scratch_shapes=[pltpu.SemaphoreType.DMA((5,))],
        compiler_params=pltpu.CompilerParams(vmem_limit_bytes=2**20),
        name="hand_over",
    )(*[pltpu.with_memory_space_constraint(value, pltpu.VMEM) for value in made])
    return outputs, grad_in, grad_w_in, grad_bias, grad_w_out


def solution(mesh):
    in_specs = (P("col", "row"), P("row", "col"), P("col"), P("col", "row"), P("col", "row"))
    out_specs = (P("col", "row"), P("col", "row"), P("row", "col"), P("col"), P("col", "row"))
    return jax.shard_map(
        on_device, mesh=mesh, in_specs=in_specs, out_specs=out_specs, check_vma=False
    )
```

time: 169 us -> 167 us (0.988)
  Pallas kernels: 167 us -> 165 us
    pallas_call x1, Pallas kernels: 165 us -> 162 us  [on_device(): pl.pallas_call(kernel, out_shape=[pltpu.VMEM(shape.shape, shape.dtype) fo...]
where the time goes in v3:
time: 167 us; the launch traced here: 166 us
  Pallas kernels  165 us (99%)
    pallas_call x1, Pallas kernels, on_device(): pl.pallas_call(kernel, out_shape=[pltpu.VMEM(shape.shape, shape.dtype) fo...  162 us

profile of v3, /device:TPU:64, one launch (start us, length us, event | category | flops | bytes accessed | tf_op | source)
XLA Modules:
  0.0 165.6 jit_solution(2338769398239725788)
XLA Ops:
  0.6 162.5 %mlp.1 = (f32[32,768]{1,0:T(8,128)S(1)}, f32[32,768]{1,0:T(8,128)S(1)}, f32[768,768]{1,0:T(8,128)S(1)}, f32[768]{0:T(1024)S(1)}, f32[768,768]{1,0:T(8,128)S(1)}) custom-call(f32[32,768]{1,0:T(8,128)} %inputs.1, f32[768,768]{1,0:T(8,128)} %in_weight.1, f32[768]{0:T(1024)} %in_bias.1, f32[768,768]{1,0:T(8,128)} %out_weight.1, f32[32,768]{1,0:T(8,128)} %out_grad.1), custom_call_target="tpu_custom_call" | custom-call | tf_op jit(solution)/shard_map/mlp/pallas_call | solution.py:398
  163.1 2.3 %hand_over.1 = (f32[32,768]{1,0:T(8,128)}, f32[32,768]{1,0:T(8,128)}, f32[768,768]{1,0:T(8,128)}, f32[768]{0:T(1024)}, f32[768,768]{1,0:T(8,128)}) custom-call(f32[32,768]{1,0:T(8,128)S(1)} %get-tuple-element.10.refs_0_, f32[32,768]{1,0:T(8,128)S(1)} %get-tuple-element.11.refs_1_, f32[768,768]{1,0:T(8,128)S(1)} %get-tuple-element.12.refs_2_, ...), custom_call_target="tpu_custom_call" | custom-call | tf_op jit(solution)/shard_map/hand_over/pallas_call | solution.py:419

commit v4 on v3

--- a/solution.py
+++ b/solution.py
@@ -166,14 +166,14 @@
         when(inside(u), own_copies[u, a].wait)
         arrived(u, "z", a, only=outside(u))
         block = units[u][0].at[a, y, x]
-        for o in (1, 3, 2):
+        for o in (2, 1, 3):
             send((u, "x", a, o), block, block, device(dx=o) if a == 0 else device(dy=o))
 
     def gather_second(u, a):
         for o in (1, 2, 3):
             arrived(u, "x", a, o)
         block = units[u][0].at[0, y] if a == 0 else units[u][0].at[1, :, x]
-        for o in (1, 3, 2):
+        for o in (2, 1, 3):
             send((u, "y", a, o), block, block, device(dy=o) if a == 0 else device(dx=o))
 
     def prepare(which):
@@ -278,7 +278,7 @@
             partial[a, :, :, :, :, columns] = value.reshape(*shape, TILE)
 
         tiles(body)
-        for o in (1, 3, 2):
+        for o in (2, 1, 3):
             if a == 0:
                 block, to = partial.at[0, lax.rem(y + o, 4)], device(dy=o)
             else:
@@ -319,7 +319,7 @@
             arrived(u, "r", a, o)
         own = partial[0, y] if a == 0 else partial[1, :, x]
         first[a, 0] = own + first[a, 0] + (first[a, 1] + first[a, 2])
-        for o in (1, 3, 2):
+        for o in (2, 1, 3):
             if a == 0:
                 block, to = first.at[0, 0, lax.rem(x + o, 4)], device(dx=o)
             else:

time: 167 us -> 165 us (0.988)
  Pallas kernels: 165 us -> 163 us
    pallas_call x1, Pallas kernels: 162 us -> 160 us  [on_device(): pl.pallas_call(kernel, out_shape=[pltpu.VMEM(shape.shape, shape.dtype) fo...]
where the time goes in v4:
time: 165 us; the launch traced here: 164 us
  Pallas kernels  163 us (99%)
    pallas_call x1, Pallas kernels, on_device(): pl.pallas_call(kernel, out_shape=[pltpu.VMEM(shape.shape, shape.dtype) fo...  160 us

profile of v4, /device:TPU:64, one launch (start us, length us, event | category | flops | bytes accessed | tf_op | source)
XLA Modules:
  0.0 163.5 jit_solution(4892921516225947291)
XLA Ops:
  0.6 160.4 %mlp.1 = (f32[32,768]{1,0:T(8,128)S(1)}, f32[32,768]{1,0:T(8,128)S(1)}, f32[768,768]{1,0:T(8,128)S(1)}, f32[768]{0:T(1024)S(1)}, f32[768,768]{1,0:T(8,128)S(1)}) custom-call(f32[32,768]{1,0:T(8,128)} %inputs.1, f32[768,768]{1,0:T(8,128)} %in_weight.1, f32[768]{0:T(1024)} %in_bias.1, f32[768,768]{1,0:T(8,128)} %out_weight.1, f32[32,768]{1,0:T(8,128)} %out_grad.1), custom_call_target="tpu_custom_call" | custom-call | tf_op jit(solution)/shard_map/mlp/pallas_call | solution.py:398
  161.1 2.3 %hand_over.1 = (f32[32,768]{1,0:T(8,128)}, f32[32,768]{1,0:T(8,128)}, f32[768,768]{1,0:T(8,128)}, f32[768]{0:T(1024)}, f32[768,768]{1,0:T(8,128)}) custom-call(f32[32,768]{1,0:T(8,128)S(1)} %get-tuple-element.10.refs_0_, f32[32,768]{1,0:T(8,128)S(1)} %get-tuple-element.11.refs_1_, f32[768,768]{1,0:T(8,128)S(1)} %get-tuple-element.12.refs_2_, ...), custom_call_target="tpu_custom_call" | custom-call | tf_op jit(solution)/shard_map/hand_over/pallas_call | solution.py:419
